TPU v7x, 128 devices: a whole 4x4x4 slice. The times are simulated.
128 devices in a mesh: grp: 2 (over x_hi), seq: 64 (over z, x_lo, y, core).
Axes of the slice: x: 4 (x_hi: 2, x_lo: 2; x = x_hi * 2 + x_lo), y: 4, z: 4, core: 2. Of those that a mesh axis runs over, the one named last changes fastest.
Arguments:
- queries: bfloat16 [32, 16384, 128], P(None, ('grp', 'seq')), may hold values from -5 to 5
- keys: bfloat16 [32, 16384, 128], P(None, ('grp', 'seq')), may hold values from -5 to 5
- values: bfloat16 [32, 16384, 128], P(None, ('grp', 'seq')), may hold values from -4 to 4
- tiles: int32 [128, 32, 38], P(('grp', 'seq')), may hold values from 0 to 127, as said below
Outputs:
- attended: bfloat16 [32, 16384, 128], P(None, ('grp', 'seq'))
Inputs may be any that keep to these rules, and one draw needn't show every extreme that they name: `tiles`: for every query band and head, columns g * 19 to (g + 1) * 19 - 1 name 19 different key bands, all from g * 64 to (g + 1) * 64 - 1.
All inputs are finite; a program needn't handle non-finite values.
Results may differ from a plain program's by a relative error of at most 0.005.
Values may be sent and summed in bfloat16 or wider, within the bound.
A program may use at most 128 MiB of HBM per device.

v0:
```python
import math

import jax
import jax.numpy as jnp
from jax import lax
from jax.sharding import PartitionSpec as P

BAND = 128


NEG_FILL = -1e30


def sent_together(arrays, axis, split_dim, concat_dim, along):
    widths = [a.shape[along] for a in arrays]
    both = jnp.concatenate(arrays, axis=along)
    whole = lax.all_to_all(both, axis, split_axis=split_dim, concat_axis=concat_dim, tiled=True)
    return tuple(jnp.split(whole, [sum(widths[:k]) for k in range(1, len(widths))], axis=along))


def from_partner(array, axis, distance):
    return lax.ppermute(array, axis, [(i, i ^ 1 << distance) for i in range(lax.axis_size(axis))])


def passed_along(block, axis, distance):
    devices = range(lax.axis_size(axis))
    route = [((i - distance) % len(devices), i) for i in devices]
    return lax.ppermute(block, axis, route)


def merge_states(first_state, second_state):
    max_first, sum_first, accum_first = first_state
    max_second, sum_second, accum_second = second_state
    joint_max = jnp.maximum(max_first, max_second)
    factor_first = jnp.exp(max_first - joint_max)
    factor_second = jnp.exp(max_second - joint_max)
    return (
        joint_max,
        sum_first * factor_first + sum_second * factor_second,
        accum_first * factor_first[..., None] + accum_second * factor_second[..., None],
    )


def attend(query_units, unit_lists, slab_keys, slab_values, group_index, group_count, carried):
    local_heads, unit_count, unit_rows, head_width = query_units.shape
    per_group = unit_lists.shape[2] // group_count
    group_bands = slab_keys.shape[1] // BAND
    block_units = math.gcd(unit_count, max(1, 512 // unit_rows))
    block_count = unit_count // block_units
    chosen = (
        lax.dynamic_slice_in_dim(unit_lists, group_index * per_group, per_group, 2)
        - group_index * group_bands
    )
    score_scale = head_width ** (-0.5)
    running_max, running_sum, accumulated = carried
    key_bands = slab_keys[0].reshape(group_bands, BAND, head_width)
    value_bands = slab_values[0].reshape(group_bands, BAND, head_width)

    def one_block(inputs):
        query_block, index_block, block_max, block_sum, block_accum = inputs
        flat_index = index_block.reshape(block_units * per_group)
        picked_keys = jnp.take(key_bands, flat_index, axis=0).reshape(
            block_units, per_group * BAND, head_width
        )
        picked_values = jnp.take(value_bands, flat_index, axis=0).reshape(
            block_units, per_group * BAND, head_width
        )
        scores = (
            jnp.einsum("urd,ukd->urk", query_block, picked_keys, preferred_element_type=jnp.float32)
            * score_scale
        )
        new_max = jnp.maximum(block_max, jnp.max(scores, axis=-1))
        factor = jnp.exp(block_max - new_max)
        weights = jnp.exp(scores - new_max[..., None])
        new_sum = block_sum * factor + jnp.sum(weights, axis=-1)
        product = jnp.einsum(
            "urk,ukd->urd",
            weights.astype(jnp.bfloat16),
            picked_values,
            preferred_element_type=jnp.float32,
        )
        return (new_max, new_sum, block_accum * factor[..., None] + product)

    def blocked(array):
        return array.reshape((block_count, block_units) + array.shape[1:])

    mapped = lax.map(
        one_block,
        (
            blocked(query_units[0]),
            blocked(chosen[0]),
            blocked(running_max[0]),
            blocked(running_sum[0]),
            blocked(accumulated[0]),
        ),
    )
    result_sets = [[piece.reshape((unit_count,) + piece.shape[2:]) for piece in mapped]]
    return (
        jnp.stack([entry[0] for entry in result_sets]),
        jnp.stack([entry[1] for entry in result_sets]),
        jnp.stack([entry[2] for entry in result_sets]),
    )


def on_device(queries, keys, values, tiles):
    head_count, tok_rows, head_width = queries.shape
    seq_count = lax.axis_size("seq")
    grp_count = lax.axis_size("grp")
    pair_count = max(1, seq_count // head_count)
    local_heads = max(1, head_count // seq_count)
    part_rows = tok_rows // pair_count
    unit_rows = min(BAND, part_rows)
    unit_per_source = part_rows // unit_rows
    dev_rows = head_count * tok_rows // seq_count
    seq_index = lax.axis_index("seq")
    grp_index = lax.axis_index("grp")
    query_sent, key_sent, value_sent = sent_together(
        (
            queries.reshape(seq_count, dev_rows, head_width),
            keys.reshape(seq_count, dev_rows, head_width),
            values.reshape(seq_count, dev_rows, head_width),
        ),
        "seq",
        0,
        0,
        1,
    )
    band_count = tiles.shape[0]
    listed = tiles.shape[2]
    by_head = jnp.transpose(tiles, (1, 0, 2)).reshape(head_count, band_count * listed)
    by_head = jnp.repeat(by_head, pair_count, axis=0).reshape(
        seq_count, local_heads, band_count * listed
    )
    lists_sent = lax.all_to_all(by_head, "seq", split_axis=0, concat_axis=0, tiled=True)
    lists_sent = lists_sent.reshape(seq_count, local_heads, band_count, listed)
    unit_lists = jnp.transpose(lists_sent, (1, 0, 2, 3)).reshape(
        local_heads, seq_count * unit_per_source, listed
    )
    query_units = jnp.transpose(
        query_sent.reshape(seq_count, local_heads, part_rows, head_width), (1, 0, 2, 3)
    )
    key_half = key_sent.reshape(seq_count, local_heads, part_rows, head_width)
    value_half = value_sent.reshape(seq_count, local_heads, part_rows, head_width)
    other_keys, other_values = from_partner((key_half, value_half), "seq", 0)
    lower_first = seq_index % 2 == 0
    key_full = jnp.concatenate(
        [
            jnp.where(lower_first, key_half, other_keys),
            jnp.where(lower_first, other_keys, key_half),
        ],
        axis=2,
    )
    value_full = jnp.concatenate(
        [
            jnp.where(lower_first, value_half, other_values),
            jnp.where(lower_first, other_values, value_half),
        ],
        axis=2,
    )
    group_keys = jnp.transpose(key_full, (1, 0, 2, 3)).reshape(
        local_heads, seq_count * tok_rows, head_width
    )
    group_values = jnp.transpose(value_full, (1, 0, 2, 3)).reshape(
        local_heads, seq_count * tok_rows, head_width
    )
    unit_count = query_units.shape[1]
    initial = (
        jnp.full((local_heads, unit_count, unit_rows), NEG_FILL, jnp.float32),
        jnp.zeros((local_heads, unit_count, unit_rows), jnp.float32),
        jnp.zeros((local_heads, unit_count, unit_rows, head_width), jnp.float32),
    )
    final_state = attend(
        query_units, unit_lists, group_keys, group_values, grp_index, grp_count, initial
    )
    guest_queries = passed_along(query_units, "grp", 1)
    guest_lists = passed_along(unit_lists, "grp", 1)
    guest_max, guest_sum, guest_accum = attend(
        guest_queries, guest_lists, group_keys, group_values, grp_index, grp_count, initial
    )
    back_state = passed_along((guest_max, guest_sum, guest_accum), "grp", -1)
    final_state = merge_states(final_state, back_state)
    running_max, running_sum, accumulated = final_state
    mixed = (accumulated / running_sum[..., None]).astype(jnp.bfloat16)
    mixed = jnp.transpose(mixed, (1, 0, 2, 3))
    mixed = mixed.reshape(seq_count, dev_rows, head_width)
    returned = lax.all_to_all(mixed, "seq", split_axis=0, concat_axis=0, tiled=True)
    return returned.reshape(head_count, tok_rows, head_width)


def solution(mesh):
    return jax.shard_map(
        on_device,
        mesh=mesh,
        in_specs=(
            P(None, ("grp", "seq"), None),
            P(None, ("grp", "seq"), None),
            P(None, ("grp", "seq"), None),
            P(("grp", "seq"), None, None),
        ),
        out_specs=P(None, ("grp", "seq"), None),
        check_vma=False,
    )
```

profile of v0, /device:TPU:1, one launch (start us, length us, event | category | flops | bytes accessed | tf_op | source)
XLA Modules:
  0.0 565.0 jit_solution(3601570343598130125)
XLA Ops:
  2.0 51.1 %all_to_all.15 = bf16[64,192,128]{2,1,0:T(8,128)(2,1)S(1)} all-to-all(bf16[64,192,128]{2,1,0:T(8,128)(2,1)S(1)} %pad_maximum_fusion), channel_id=1, replica_groups=mesh['grp'=2,'seq'=64] {'seq'}, dimensions={0} | all-to-all | bytes 6291456 | tf_op jit(solution)/shard_map/all_to_all | solution.py:17
  65.8 19.5 %all-to-all-done.1 = s32[64,1,38]{2,1,0:T(1,128)S(1)} async-done(((s32[64,1,38]{2,1,0:T(1,128)}), s32[64,1,38]{2,1,0:T(1,128)S(1)}, u32[]{:S(2)}, u32[]{:S(2)}) %all-to-all-start.1) | async-done | bytes 9760 | tf_op jit(solution)/shard_map/all_to_all | solution.py:134
  95.1 220.0 %while.29 = (s32[]{:T(128)}, f32[8,8,64]{2,1,0:T(8,128)S(1)}, f32[8,8,64]{2,1,0:T(8,128)S(1)}, f32[8,8,64,128]{3,2,1,0:T(8,128)}, bf16[8,8,64,128]{3,2,1,0:T(8,1...) while((s32[]{:T(128)}, f32[8,8,64]{2,1,0:T(8,128)S(1)}, ...), condition=%wide.region_7.9_spmd, body=%wide.region_4.8_spmd.sunk | while | flops 650056576 | bytes 65187156 | solution.py:87
  95.2 9.2 %gather_fusion.2 = bf16[152,128,128]{2,1,0:T(8,128)(2,1)} fusion(bf16[64,128,128]{2,1,0:T(8,128)(2,1)} %get-tuple-element.318, s32[1024]{0:T(1024)S(1)} %pad_clamp_fusion.5), kind=kCustom, calls=%fused_computation.3.clone.clone.1 | custom fusion | bytes 9962080 | tf_op jit(solution)/shard_map/while/body/eval_jaxpr/jit(_take)/gather | solution.py:65
  104.4 7.6 %gather_fusion.3 = bf16[152,128,128]{2,1,0:T(8,128)(2,1)} fusion(bf16[64,128,128]{2,1,0:T(8,128)(2,1)S(1)} %get-tuple-element.317, s32[1024]{0:T(1024)S(1)} %pad_clamp_fusion.5), kind=kCustom, calls=%fused_computation.2.clone.clone.1 | custom fusion | bytes 9962080 | tf_op jit(solution)/shard_map/while/body/eval_jaxpr/jit(_take)/gather | solution.py:62
  122.7 9.2 %gather_fusion.2 = bf16[152,128,128]{2,1,0:T(8,128)(2,1)} fusion(bf16[64,128,128]{2,1,0:T(8,128)(2,1)} %get-tuple-element.318, s32[1024]{0:T(1024)S(1)} %pad_clamp_fusion.5), kind=kCustom, calls=%fused_computation.3.clone.clone.1 | custom fusion | bytes 9962080 | tf_op jit(solution)/shard_map/while/body/eval_jaxpr/jit(_take)/gather | solution.py:65
  150.2 9.2 %gather_fusion.2 = bf16[152,128,128]{2,1,0:T(8,128)(2,1)} fusion(bf16[64,128,128]{2,1,0:T(8,128)(2,1)} %get-tuple-element.318, s32[1024]{0:T(1024)S(1)} %pad_clamp_fusion.5), kind=kCustom, calls=%fused_computation.3.clone.clone.1 | custom fusion | bytes 9962080 | tf_op jit(solution)/shard_map/while/body/eval_jaxpr/jit(_take)/gather | solution.py:65
  177.7 9.2 %gather_fusion.2 = bf16[152,128,128]{2,1,0:T(8,128)(2,1)} fusion(bf16[64,128,128]{2,1,0:T(8,128)(2,1)} %get-tuple-element.318, s32[1024]{0:T(1024)S(1)} %pad_clamp_fusion.5), kind=kCustom, calls=%fused_computation.3.clone.clone.1 | custom fusion | bytes 9962080 | tf_op jit(solution)/shard_map/while/body/eval_jaxpr/jit(_take)/gather | solution.py:65
  205.2 9.2 %gather_fusion.2 = bf16[152,128,128]{2,1,0:T(8,128)(2,1)} fusion(bf16[64,128,128]{2,1,0:T(8,128)(2,1)} %get-tuple-element.318, s32[1024]{0:T(1024)S(1)} %pad_clamp_fusion.5), kind=kCustom, calls=%fused_computation.3.clone.clone.1 | custom fusion | bytes 9962080 | tf_op jit(solution)/shard_map/while/body/eval_jaxpr/jit(_take)/gather | solution.py:65
  232.7 9.2 %gather_fusion.2 = bf16[152,128,128]{2,1,0:T(8,128)(2,1)} fusion(bf16[64,128,128]{2,1,0:T(8,128)(2,1)} %get-tuple-element.318, s32[1024]{0:T(1024)S(1)} %pad_clamp_fusion.5), kind=kCustom, calls=%fused_computation.3.clone.clone.1 | custom fusion | bytes 9962080 | tf_op jit(solution)/shard_map/while/body/eval_jaxpr/jit(_take)/gather | solution.py:65
  260.2 9.2 %gather_fusion.2 = bf16[152,128,128]{2,1,0:T(8,128)(2,1)} fusion(bf16[64,128,128]{2,1,0:T(8,128)(2,1)} %get-tuple-element.318, s32[1024]{0:T(1024)S(1)} %pad_clamp_fusion.5), kind=kCustom, calls=%fused_computation.3.clone.clone.1 | custom fusion | bytes 9962080 | tf_op jit(solution)/shard_map/while/body/eval_jaxpr/jit(_take)/gather | solution.py:65
  287.7 9.2 %gather_fusion.2 = bf16[152,128,128]{2,1,0:T(8,128)(2,1)} fusion(bf16[64,128,128]{2,1,0:T(8,128)(2,1)} %get-tuple-element.318, s32[1024]{0:T(1024)S(1)} %pad_clamp_fusion.5), kind=kCustom, calls=%fused_computation.3.clone.clone.1 | custom fusion | bytes 9962080 | tf_op jit(solution)/shard_map/while/body/eval_jaxpr/jit(_take)/gather | solution.py:65
  321.4 212.7 %while.28 = (s32[]{:T(128)}, f32[8,8,64]{2,1,0:T(8,128)S(1)}, f32[8,8,64]{2,1,0:T(8,128)S(1)}, f32[8,8,64,128]{3,2,1,0:T(8,128)}, bf16[8,8,64,128]{3,2,1,0:T(8,1...) while((s32[]{:T(128)}, f32[8,8,64]{2,1,0:T(8,128)S(1)}, ...), condition=%wide.region_3.5_spmd, body=%wide.region_0.4_spmd.sunk | while | flops 650056576 | bytes 65186648 | solution.py:87
  321.6 9.2 %gather_fusion = bf16[152,128,128]{2,1,0:T(8,128)(2,1)} fusion(bf16[64,128,128]{2,1,0:T(8,128)(2,1)} %get-tuple-element.345, s32[1024]{0:T(1024)S(1)} %pad_clamp_fusion.4), kind=kCustom, calls=%fused_computation.1.clone.clone.1 | custom fusion | bytes 9962080 | tf_op jit(solution)/shard_map/while/body/eval_jaxpr/jit(_take)/gather | solution.py:65
  348.1 9.2 %gather_fusion = bf16[152,128,128]{2,1,0:T(8,128)(2,1)} fusion(bf16[64,128,128]{2,1,0:T(8,128)(2,1)} %get-tuple-element.345, s32[1024]{0:T(1024)S(1)} %pad_clamp_fusion.4), kind=kCustom, calls=%fused_computation.1.clone.clone.1 | custom fusion | bytes 9962080 | tf_op jit(solution)/shard_map/while/body/eval_jaxpr/jit(_take)/gather | solution.py:65
  357.4 7.6 %gather_fusion.1 = bf16[152,128,128]{2,1,0:T(8,128)(2,1)} fusion(bf16[64,128,128]{2,1,0:T(8,128)(2,1)S(1)} %get-tuple-element.344, s32[1024]{0:T(1024)S(1)} %pad_clamp_fusion.4), kind=kCustom, calls=%fused_computation.clone.clone.1 | custom fusion | bytes 9962080 | tf_op jit(solution)/shard_map/while/body/eval_jaxpr/jit(_take)/gather | solution.py:62
  374.7 9.2 %gather_fusion = bf16[152,128,128]{2,1,0:T(8,128)(2,1)} fusion(bf16[64,128,128]{2,1,0:T(8,128)(2,1)} %get-tuple-element.345, s32[1024]{0:T(1024)S(1)} %pad_clamp_fusion.4), kind=kCustom, calls=%fused_computation.1.clone.clone.1 | custom fusion | bytes 9962080 | tf_op jit(solution)/shard_map/while/body/eval_jaxpr/jit(_take)/gather | solution.py:65
  401.3 9.2 %gather_fusion = bf16[152,128,128]{2,1,0:T(8,128)(2,1)} fusion(bf16[64,128,128]{2,1,0:T(8,128)(2,1)} %get-tuple-element.345, s32[1024]{0:T(1024)S(1)} %pad_clamp_fusion.4), kind=kCustom, calls=%fused_computation.1.clone.clone.1 | custom fusion | bytes 9962080 | tf_op jit(solution)/shard_map/while/body/eval_jaxpr/jit(_take)/gather | solution.py:65
  427.9 9.2 %gather_fusion = bf16[152,128,128]{2,1,0:T(8,128)(2,1)} fusion(bf16[64,128,128]{2,1,0:T(8,128)(2,1)} %get-tuple-element.345, s32[1024]{0:T(1024)S(1)} %pad_clamp_fusion.4), kind=kCustom, calls=%fused_computation.1.clone.clone.1 | custom fusion | bytes 9962080 | tf_op jit(solution)/shard_map/while/body/eval_jaxpr/jit(_take)/gather | solution.py:65
  454.5 9.2 %gather_fusion = bf16[152,128,128]{2,1,0:T(8,128)(2,1)} fusion(bf16[64,128,128]{2,1,0:T(8,128)(2,1)} %get-tuple-element.345, s32[1024]{0:T(1024)S(1)} %pad_clamp_fusion.4), kind=kCustom, calls=%fused_computation.1.clone.clone.1 | custom fusion | bytes 9962080 | tf_op jit(solution)/shard_map/while/body/eval_jaxpr/jit(_take)/gather | solution.py:65
  481.1 9.2 %gather_fusion = bf16[152,128,128]{2,1,0:T(8,128)(2,1)} fusion(bf16[64,128,128]{2,1,0:T(8,128)(2,1)} %get-tuple-element.345, s32[1024]{0:T(1024)S(1)} %pad_clamp_fusion.4), kind=kCustom, calls=%fused_computation.1.clone.clone.1 | custom fusion | bytes 9962080 | tf_op jit(solution)/shard_map/while/body/eval_jaxpr/jit(_take)/gather | solution.py:65
  507.7 9.2 %gather_fusion = bf16[152,128,128]{2,1,0:T(8,128)(2,1)} fusion(bf16[64,128,128]{2,1,0:T(8,128)(2,1)} %get-tuple-element.345, s32[1024]{0:T(1024)S(1)} %pad_clamp_fusion.4), kind=kCustom, calls=%fused_computation.1.clone.clone.1 | custom fusion | bytes 9962080 | tf_op jit(solution)/shard_map/while/body/eval_jaxpr/jit(_take)/gather | solution.py:65
  516.9 7.6 %gather_fusion.1 = bf16[152,128,128]{2,1,0:T(8,128)(2,1)} fusion(bf16[64,128,128]{2,1,0:T(8,128)(2,1)S(1)} %get-tuple-element.344, s32[1024]{0:T(1024)S(1)} %pad_clamp_fusion.4), kind=kCustom, calls=%fused_computation.clone.clone.1 | custom fusion | bytes 9962080 | tf_op jit(solution)/shard_map/while/body/eval_jaxpr/jit(_take)/gather | solution.py:62
  538.1 25.9 %all_to_all.16 = bf16[64,64,128]{2,1,0:T(8,128)(2,1)S(1)} all-to-all(bf16[64,64,128]{2,1,0:T(8,128)(2,1)S(1)} %fusion.43), channel_id=1, replica_groups=mesh['grp'=2,'seq'=64] {'seq'}, dimensions={0} | all-to-all | bytes 2097152 | tf_op jit(solution)/shard_map/all_to_all | solution.py:186
  (224 shorter events, 297.3 us)
Async XLA Ops:
  53.1 1.6 copy-start
  54.8 5.5 copy-start.1
  57.3 32.4 %collective-permute-start = (bf16[64,1,64,128]{3,2,0,1:T(8,128)(2,1)}, bf16[64,1,64,128]{3,2,0,1:T(8,128)(2,1)S(1)}, u32[]{:S(2)}, u32[]{:S(2)}) collective-permute-start(bf16[64,1,64,128]{3,2,0,1:T(8,128)(2,1)} %get-tuple-element.154), channel_id=1, source_target_pairs={{0,1},{1,0},{2,3},{3,2},{4,5},{5,4},{6,7},{7,6},{8,9},{9,8},{10,11... | collective-permute-start | bytes 3145736 | tf_op jit(solution)/shard_map/ppermute | solution.py:22
  57.6 32.1 %collective-permute-start.1 = (bf16[64,1,64,128]{3,2,0,1:T(8,128)(2,1)S(1)}, bf16[64,1,64,128]{3,2,0,1:T(8,128)(2,1)}, u32[]{:S(2)}, u32[]{:S(2)}) collective-permute-start(bf16[64,1,64,128]{3,2,0,1:T(8,128)(2,1)S(1)} %get-tuple-element.153), channel_id=1, source_target_pairs={{0,1},{1,0},{2,3},{3,2},{4,5},{5,4},{6,7},{7,6},{8,9},{9,8},{10,11... | collective-permute-start | bytes 3145736 | tf_op jit(solution)/shard_map/ppermute | solution.py:22
  57.8 35.7 %collective-permute-start.2 = (bf16[1,64,64,128]{3,2,1,0:T(8,128)(2,1)}, bf16[1,64,64,128]{3,2,1,0:T(8,128)(2,1)}, u32[]{:S(2)}, u32[]{:S(2)}) collective-permute-start(bf16[1,64,64,128]{3,2,1,0:T(8,128)(2,1)} %get-tuple-element.152), channel_id=1, source_target_pairs={{64,0},{0,64},{65,1},{1,65},{66,2},{2,66},{67,3},{3,67},{68,4},{4,... | collective-permute-start | bytes 3145736 | tf_op jit(solution)/shard_map/ppermute | solution.py:28
  60.9 24.5 %all-to-all-start.1 = ((s32[64,1,38]{2,1,0:T(1,128)}), s32[64,1,38]{2,1,0:T(1,128)S(1)}, u32[]{:S(2)}, u32[]{:S(2)}) async-start(s32[64,1,38]{2,1,0:T(1,128)} %bitcast.17), calls=%async_computation.1 | async-start | bytes 65536 | tf_op jit(solution)/shard_map/all_to_all | solution.py:134
  85.3 4.3 collective-permute-start.3
  315.1 219.1 %collective-permute-start.4 = (f32[1,64,64]{2,1,0:T(8,128)S(1)}, f32[1,64,64]{2,1,0:T(8,128)S(1)}, u32[]{:S(2)}, u32[]{:S(2)}) collective-permute-start(f32[1,64,64]{2,1,0:T(8,128)S(1)} %bitcast.166), channel_id=1, source_target_pairs={{64,0},{0,64},{65,1},{1,65},{66,2},{2,66},{67,3},{3,67},{68,4},{4,... | collective-permute-start | bytes 49160 | tf_op jit(solution)/shard_map/ppermute | solution.py:28
  316.8 217.3 %collective-permute-start.6 = (f32[1,64,64]{2,1,0:T(8,128)S(1)}, f32[1,64,64]{2,1,0:T(8,128)S(1)}, u32[]{:S(2)}, u32[]{:S(2)}) collective-permute-start(f32[1,64,64]{2,1,0:T(8,128)S(1)} %bitcast.167), channel_id=1, source_target_pairs={{64,0},{0,64},{65,1},{1,65},{66,2},{2,66},{67,3},{3,67},{68,4},{4,... | collective-permute-start | bytes 49160 | tf_op jit(solution)/shard_map/ppermute | solution.py:28
  318.1 216.1 %collective-permute-start.5 = (f32[1,64,64,128]{3,2,1,0:T(8,128)}, f32[1,64,64,128]{3,2,1,0:T(8,128)}, u32[]{:S(2)}, u32[]{:S(2)}) collective-permute-start(f32[1,64,64,128]{3,2,1,0:T(8,128)} %bitcast.160), channel_id=1, source_target_pairs={{64,0},{0,64},{65,1},{1,65},{66,2},{2,66},{67,3},{3,67},{68,4},{4,... | collective-permute-start | bytes 6291464 | tf_op jit(solution)/shard_map/ppermute | solution.py:28
where the time goes:
time: 566 us; the launch traced here: 565 us
  local copies, waits for them, and re-layouts  280 us (49%)
  other arithmetic  102 us (18%)
  blocking collectives  77 us (14%)
  matrix products  69.2 us (12%)
  waiting for transfers between devices  21.9 us (4%)
  starting transfers between devices  14.4 us (3%)
    gather x16, local copies, waits for them, and re-layouts, one_block(): jnp.take(value_bands, flat_index, axis=0)  147 us
    gather x16, local copies, waits for them, and re-layouts, one_block(): jnp.take(key_bands, flat_index, axis=0)  122 us
    select_n x16, other arithmetic, one_block(): jnp.take(value_bands, flat_index, axis=0)  78.5 us
    all_to_all x1, blocking collectives, sent_together(): lax.all_to_all(both, axis, split_axis=split_dim, concat_axis=concat_dim,...  51.1 us
    dot_general x16, matrix products, one_block(): jnp.einsum('urd,ukd->urk', query_block, picked_keys, preferred_element_ty...  39.2 us
    dot_general x16, matrix products, one_block(): jnp.einsum('urk,ukd->urd', weights.astype(jnp.bfloat16), picked_values, p...  30 us
    all_to_all x1, blocking collectives, on_device(): lax.all_to_all(mixed, 'seq', split_axis=0, concat_axis=0, tiled=True)  25.9 us
    all_to_all x1, waiting for transfers between devices, on_device(): lax.all_to_all(by_head, 'seq', split_axis=0, concat_axis=0, tiled=True)  19.5 us
  transfers between devices with their start and end apart: 8, of which 2 were waited for; matrix products, arithmetic and copies ran while one was open for 39% of the time, Pallas kernels for 0%

commit v1 on v0

v1 whole, which is shorter than its diff:
```python
import functools

import jax
import jax.numpy as jnp
from jax import lax
from jax.experimental import pallas as pl
from jax.experimental.pallas import tpu as pltpu
from jax.sharding import PartitionSpec as P

MESH = pl.DeviceIdType.MESH
BAND = 128
WIDTH = 128
HEADS = 32
PER = 19
SCALE = 128.0**-0.5 * 1.4426950408889634
NT = (((1,), (1,)), ((), ()))
COLS = [list(range(i, min(PER, i + 2))) for i in range(0, PER, 2)]


def device(x, y, z, c):
    return (x // 2, ((z * 2 + x % 2) * 4 + y) * 2 + c)


def kernel(
    q_ref, k_ref, v_ref, tiles_ref, o_ref,
    own_kv, far_kv, queries, lists_out, lists_in, lists, scores, maxima, acc_own, max_own, mixed,
    send_kv, send_lists, send_fwd, send_out,
    got_direct, got_partner, got_sibling, got_relayed, got_queries, got_lists, got_out, lists_sem,
):
    s = lax.axis_index("seq")
    pair = lax.axis_index("grp")
    c = s % 2
    y = (s // 2) % 4
    x_lo = (s // 8) % 2
    z = s // 16
    x = pair * 2 + x_lo
    beside = 3 - x
    sibling = device(x, y, z, 1 - c)
    partner = device(x + 1 - 2 * x_lo, y, z, c)
    own_head = pair * 16 + z * 4 + y
    own_part = (x_lo * 2 + c) * 16
    far_part = ((1 - x_lo) * 2 + c) * 16

    t = tiles_ref[0]
    head = lax.broadcasted_iota(jnp.int32, t.shape, 0)
    dy_of = ((head & 3) - ((t >> 1) & 3)) & 3
    dz_of = (((head >> 2) & 3) - ((t >> 4) & 3)) & 3
    slot_of = (((t >> 3) & 1) * 2 + (t & 1)) * 16 + ((dz_of - dy_of) & 3) * 4 + dy_of
    slot_of = jnp.concatenate([slot_of, jnp.zeros((HEADS, 128 - 2 * PER), jnp.int32)], 1)
    for h in range(HEADS):
        lists_out[h] = slot_of[h : h + 1]

    def target(i):
        dy = i % 4
        dz = (i // 4 + dy) % 4
        return (y + dy) % 4, (z + dz) % 4

    def remote(src, dst, send_sem, recv_sem, device_id):
        return pltpu.make_async_remote_copy(
            src_ref=src, dst_ref=dst, send_sem=send_sem, recv_sem=recv_sem, device_id=device_id, device_id_type=MESH
        )

    def send_lists_to(i, own):
        ty, tz = target(i)
        if own:
            remote(lists_out.at[pair * 16 + tz * 4 + ty], lists_in.at[i], send_lists, got_lists, device(x, ty, tz, c)).start()
        remote(
            lists_out.at[(1 - pair) * 16 + tz * 4 + ty], lists_in.at[16 + i], send_lists, got_lists, device(beside, ty, tz, c)
        ).start()

    def send_kv_to(i, own):
        ty, tz = target(i)
        here, there = pair * 16 + tz * 4 + ty, (1 - pair) * 16 + tz * 4 + ty
        for which, ref in ((0, k_ref), (1, v_ref)):
            if own:
                remote(
                    ref.at[here], own_kv.at[own_part + i, which], send_kv, got_direct.at[0, i // 4], device(x, ty, tz, c)
                ).start()
            remote(
                ref.at[there], far_kv.at[own_part + i, which], send_kv, got_direct.at[1, i // 4], device(beside, ty, tz, c)
            ).start()

    def send_queries_to(i, own):
        ty, tz = target(i)
        if own:
            remote(q_ref.at[pair * 16 + tz * 4 + ty], queries.at[i], send_kv, got_queries, device(x, ty, tz, c)).start()
        remote(
            q_ref.at[(1 - pair) * 16 + tz * 4 + ty], queries.at[16 + i], send_kv, got_queries, device(beside, ty, tz, c)
        ).start()

    def each_offset(step):
        step(0, False)

        def body(i, carry):
            step(i, True)
            return carry

        lax.fori_loop(1, 16, body, 0)

    pltpu.make_async_copy(k_ref.at[own_head], own_kv.at[own_part, 0], got_direct.at[0, 0]).start()
    pltpu.make_async_copy(v_ref.at[own_head], own_kv.at[own_part, 1], got_direct.at[0, 0]).start()
    pltpu.make_async_copy(q_ref.at[own_head], queries.at[0], got_queries).start()
    pltpu.make_async_copy(lists_out.at[own_head], lists_in.at[0], got_lists).start()
    each_offset(send_lists_to)
    each_offset(send_kv_to)
    each_offset(send_queries_to)

    def chunk(ref, part, j):
        return ref.at[pl.ds(part + j * 4, 4)]

    def arrived(view, sem):
        pltpu.make_async_copy(view, view, sem).wait()

    def pass_on(ref, part, plane, j):
        view = chunk(ref, part, j)
        arrived(view, got_direct.at[plane, j])
        remote(view, view, send_fwd, got_partner.at[plane, j], partner).start()
        remote(view, view, send_fwd, got_sibling.at[plane], sibling).start()

    def relay(ref, part, plane, j):
        view = chunk(ref, part, j)
        arrived(view, got_partner.at[plane, j])
        remote(view, view, send_fwd, got_relayed.at[plane], sibling).start()

    def four(step):
        def body(j, carry):
            step(j)
            return carry

        lax.fori_loop(0, 4, body, 0)

    four(lambda j: pass_on(own_kv, own_part, 0, j))
    four(lambda j: pass_on(far_kv, far_part, 1, j))
    four(lambda j: relay(own_kv, far_part, 0, j))
    arrived(lists_in, got_lists)
    copy_lists = pltpu.make_async_copy(lists_in, lists, lists_sem)
    copy_lists.start()
    copy_lists.wait()
    arrived(queries, got_queries)
    part = own_kv.at[pl.ds(0, 16)]
    arrived(part, got_sibling.at[0])
    arrived(part, got_relayed.at[0])

    def attend(kv, base, finish, between):
        def step(new, new_slot, old, old_slot):
            running = acc = None
            if new is not None:
                query = queries[new]
            if old is not None:
                shift = maxima[old_slot]
            for cols in COLS:
                span = pl.ds(cols[0] * BAND, len(cols) * BAND)
                if new is not None:
                    keys = jnp.concatenate([kv[lists[new, 0, base + col], 0] for col in cols], 0)
                    found = lax.dot_general(query, keys, NT, preferred_element_type=jnp.float32)
                    scores[new_slot, :, span] = found
                    for n in range(len(cols)):
                        piece = found[:, n * BAND : (n + 1) * BAND]
                        running = piece if running is None else jnp.maximum(running, piece)
                if old is not None:
                    values = jnp.concatenate([kv[lists[old, 0, base + col], 1] for col in cols], 0)
                    values = jnp.concatenate([values, jnp.ones_like(values)], 1)
                    weights = jnp.exp2(scores[old_slot, :, span] * SCALE - jnp.concatenate([shift] * len(cols), 1))
                    product = jnp.dot(weights.astype(jnp.bfloat16), values, preferred_element_type=jnp.float32)
                    acc = product if acc is None else acc + product
            if new is not None:
                maxima[new_slot] = jnp.broadcast_to(jnp.max(running, -1, keepdims=True) * SCALE, (BAND, BAND))
            if old is not None:
                finish(old, shift, acc)

        step(0, 0, None, None)

        def body(i, carry):
            step(2 * i + 1, 1, 2 * i, 0)
            step(jnp.minimum(2 * i + 2, 31), 0, 2 * i + 1, 1)
            between(i)
            return carry

        lax.fori_loop(0, 16, body, 0)

    def keep(unit, shift, acc):
        acc_own[unit] = acc
        max_own[unit] = shift

    def relay_between(i):
        @pl.when(i % 4 == 3)
        def _():
            relay(far_kv, own_part, 1, i // 4)

    attend(own_kv, pair * PER, keep, relay_between)

    part = far_kv.at[pl.ds(0, 16)]
    arrived(part, got_sibling.at[1])
    arrived(part, got_relayed.at[1])

    def merge(unit, shift, acc):
        first, first_shift = acc_own[unit], max_own[unit]
        joint = jnp.maximum(shift, first_shift)
        now, before = jnp.exp2(shift - joint), jnp.exp2(first_shift - joint)
        top = acc[:, :WIDTH] * now + first[:, :WIDTH] * before
        bottom = acc[:, WIDTH:] * now + first[:, WIDTH:] * before
        mixed[unit] = (top / bottom).astype(jnp.bfloat16)

    def give_back(unit):
        i = unit % 16
        dy = i % 4
        dz = (i // 4 + dy) % 4
        plane = jnp.where(unit < 16, x, beside)
        remote(
            mixed.at[unit], o_ref.at[own_head], send_out, got_out,
            device(plane, (y - dy + 4) % 4, (z - dz + 4) % 4, c),
        ).start()

    def give_two(i):
        @pl.when(i == 0)
        def _():
            pltpu.make_async_copy(mixed.at[0], o_ref.at[own_head], got_out).start()

        @pl.when(i > 0)
        def _():
            give_back(2 * i)

        give_back(2 * i + 1)

    attend(far_kv, (1 - pair) * PER, merge, give_two)

    def sent(view, sem):
        pltpu.make_async_copy(view, view, sem).wait()

    arrived(o_ref, got_out)
    sent(o_ref.at[pl.ds(0, 31)], send_out)
    sent(lists_out.at[pl.ds(0, 31)], send_lists)
    sent(own_kv.at[pl.ds(0, 31)], send_kv)
    sent(queries.at[pl.ds(0, 31)], send_kv)
    sent(own_kv, send_fwd)
    sent(own_kv.at[pl.ds(0, 32)], send_fwd)


def on_device(queries, keys, values, tiles):
    dma = pltpu.SemaphoreType.DMA
    any_space = pl.BlockSpec(memory_space=pl.ANY)
    bf16, f32 = jnp.bfloat16, jnp.float32
    return pl.pallas_call(
        kernel,
        out_shape=jax.ShapeDtypeStruct((HEADS, BAND, WIDTH), bf16),
        in_specs=[any_space, any_space, any_space, pl.BlockSpec(memory_space=pltpu.VMEM)],
        out_specs=any_space,
        scratch_shapes=[
            pltpu.VMEM((64, 2, BAND, WIDTH), bf16),
            pltpu.VMEM((64, 2, BAND, WIDTH), bf16),
            pltpu.VMEM((32, BAND, WIDTH), bf16),
            pltpu.VMEM((HEADS, 1, 128), jnp.int32),
            pltpu.VMEM((32, 1, 128), jnp.int32),
            pltpu.SMEM((32, 1, 128), jnp.int32),
            pltpu.VMEM((2, BAND, PER * BAND), f32),
            pltpu.VMEM((2, BAND, BAND), f32),
            pltpu.VMEM((32, BAND, 2 * WIDTH), f32),
            pltpu.VMEM((32, BAND, BAND), f32),
            pltpu.VMEM((32, BAND, WIDTH), bf16),
            dma, dma, dma, dma,
            dma((2, 4)), dma((2, 4)), dma((2,)), dma((2,)), dma, dma, dma, dma,
        ],
        compiler_params=pltpu.CompilerParams(has_side_effects=True, vmem_limit_bytes=52 * 2**20),
        cost_estimate=pl.CostEstimate(flops=10_200_000_000, bytes_accessed=4 * 2**20, transcendentals=20_000_000),
        name="attend_listed",
    )(queries, keys, values, tiles)


def solution(mesh):
    return jax.shard_map(
        on_device,
        mesh=mesh,
        in_specs=(
            P(None, ("grp", "seq"), None),
            P(None, ("grp", "seq"), None),
            P(None, ("grp", "seq"), None),
            P(("grp", "seq"), None, None),
        ),
        out_specs=P(None, ("grp", "seq"), None),
        check_vma=False,
    )
```

time: 566 us -> 106 us (0.19)
  local copies, waits for them, and re-layouts: 280 us -> 1.69 us
  Pallas kernels: 0 us -> 104 us
  other arithmetic: 102 us -> 0 us
  blocking collectives: 77 us -> 0 us
  matrix products: 69.2 us -> 0 us
  waiting for transfers between devices: 21.9 us -> 0 us
  starting transfers between devices: 14.4 us -> 0 us
    gather x32 -> x0, local copies, waits for them, and re-layouts: 270 us -> none  [the longest x16 147 us: one_block(): jnp.take(value_bands, flat_index, axis=0)]
    pallas_call x0 -> x1, Pallas kernels: none -> 104 us  [on_device(): pl.pallas_call(kernel, out_shape=jax.ShapeDtypeStruct((HEADS, BAND, WIDTH...]
    select_n x33 -> x0, other arithmetic: 80.8 us -> none  [the longest x16 78.5 us: one_block(): jnp.take(value_bands, flat_index, axis=0)]
    all_to_all x2 -> x0, blocking collectives: 77 us -> none  [the longest x1 51.1 us: sent_together(): lax.all_to_all(both, axis, split_axis=split_dim, concat_axis=concat_dim,...]
    dot_general x32 -> x0, matrix products: 69.2 us -> none  [the longest x16 39.2 us: one_block(): jnp.einsum('urd,ukd->urk', query_block, picked_keys, preferred_element_ty...]
    all_to_all x1 -> x0, waiting for transfers between devices: 19.5 us -> none  [on_device(): lax.all_to_all(by_head, 'seq', split_axis=0, concat_axis=0, tiled=True)]
    reduce_sum x16 -> x0, other arithmetic: 12.7 us -> none  [one_block(): new_sum = block_sum * factor + jnp.sum(weights, axis=-1)]
    ppermute x7 -> x0, starting transfers between devices: 9.47 us -> none  [the longest x5 8.96 us: passed_along(): return lax.ppermute(block, axis, route)]
  transfers between devices with their start and end apart: 8 -> 0, of which waited for: 2 -> 0; matrix products, arithmetic and copies ran while one was open for 39% -> 0% of each run, Pallas kernels for 0% -> 0%
where the time goes in v1:
time: 106 us
  Pallas kernels  104 us (98%)
  local copies, waits for them, and re-layouts  1.69 us (2%)
    pallas_call x1, Pallas kernels, on_device(): pl.pallas_call(kernel, out_shape=jax.ShapeDtypeStruct((HEADS, BAND, WIDTH...  104 us

profile of v1, /device:TPU:1, one launch (start us, length us, event | category | flops | bytes accessed | tf_op | source)
XLA Modules:
  0.0 106.1 jit_solution(4672176933826448023)
XLA Ops:
  0.0 0.0 copy-start
  0.0 0.7 copy-done
  0.7 104.4 %attend_listed.1 = bf16[32,128,128]{2,1,0:T(8,128)(2,1)S(1)} custom-call(bf16[32,128,128]{2,1,0:T(8,128)(2,1)} %q_ref.1, bf16[32,128,128]{2,1,0:T(8,128)(2,1)} %k_ref.1, bf16[32,128,128]{2,1,0:T(8,128)(2,1)} %v_ref.1, s32[1,32,38]{2,1,0:T(8,128)S(1)} %copy-done), custom_call_target="tpu_custom_call" | custom-call | flops 10200000512 | bytes 4194304 | tf_op jit(solution)/shard_map/attend_listed/pallas_call | solution.py:243
  105.1 1.0 copy.6
Async XLA Ops:
  0.0 0.7 copy-start

commit v2 on v1

v2 whole, which is shorter than its diff:
```python
import functools

import jax
import jax.numpy as jnp
from jax import lax
from jax.experimental import pallas as pl
from jax.experimental.pallas import tpu as pltpu
from jax.sharding import PartitionSpec as P

MESH = pl.DeviceIdType.MESH
BAND = 128
WIDTH = 128
HEADS = 32
PER = 19
SCALE = 128.0**-0.5 * 1.4426950408889634
NT = (((1,), (1,)), ((), ()))
OWN_K, OWN_V, FAR_K, FAR_V = range(4)
STEP = 8
COLS = [list(range(i, min(PER, i + 2))) for i in range(0, PER, 2)]


def device(x, y, z, c):
    return (x // 2, ((z * 2 + x % 2) * 4 + y) * 2 + c)


def kernel(
    q_ref, k_ref, v_ref, tiles_ref, o_ref,
    own_k, own_v, far_k, far_v, queries, lists_out, lists_in, lists, weights, acc_own, max_own, max_far, mixed,
    send_kv, send_lists, send_fwd, send_out,
    got_direct, got_partner, got_sibling, got_relayed, got_queries, got_lists, got_out, lists_sem,
):
    s = lax.axis_index("seq")
    pair = lax.axis_index("grp")
    c = s % 2
    y = (s // 2) % 4
    x_lo = (s // 8) % 2
    z = s // 16
    x = pair * 2 + x_lo
    beside = 3 - x
    sibling = device(x, y, z, 1 - c)
    partner = device(x + 1 - 2 * x_lo, y, z, c)
    own_head = pair * 16 + z * 4 + y
    own_part = (x_lo * 2 + c) * 16
    far_part = ((1 - x_lo) * 2 + c) * 16

    def target(i):
        dy = i % 4
        dz = (i // 4 + dy) % 4
        return (y + dy) % 4, (z + dz) % 4

    barrier = pltpu.get_barrier_semaphore()

    def greet(device_id):
        pl.semaphore_signal(barrier, inc=1, device_id=device_id, device_id_type=MESH)

    greet(sibling)
    greet(partner)
    greet(device(beside, y, z, c))

    def greet_both(i, carry):
        ty, tz = target(i)
        greet(device(x, ty, tz, c))
        greet(device(beside, ty, tz, c))
        return carry

    lax.fori_loop(1, 16, greet_both, 0)

    t = tiles_ref[0]
    head = lax.broadcasted_iota(jnp.int32, t.shape, 0)
    dy_of = ((head & 3) - ((t >> 1) & 3)) & 3
    dz_of = (((head >> 2) & 3) - ((t >> 4) & 3)) & 3
    slot_of = (((t >> 3) & 1) * 2 + (t & 1)) * 16 + ((dz_of - dy_of) & 3) * 4 + dy_of
    slot_of = jnp.concatenate([slot_of, jnp.zeros((HEADS, 128 - 2 * PER), jnp.int32)], 1)
    for h in range(HEADS):
        lists_out[h] = slot_of[h : h + 1]

    def remote(src, dst, send_sem, recv_sem, device_id):
        return pltpu.make_async_remote_copy(
            src_ref=src, dst_ref=dst, send_sem=send_sem, recv_sem=recv_sem, device_id=device_id, device_id_type=MESH
        )

    def send_lists_to(i, own):
        ty, tz = target(i)
        if own:
            remote(
                lists_out.at[pair * 16 + tz * 4 + ty], lists_in.at[16 + i], send_lists, got_lists, device(x, ty, tz, c)
            ).start()
        remote(
            lists_out.at[(1 - pair) * 16 + tz * 4 + ty], lists_in.at[i], send_lists, got_lists, device(beside, ty, tz, c)
        ).start()

    def send_own(kind, ref):
        def step(i, away):
            ty, tz = target(i)
            src, dst = ref.at[pair * 16 + tz * 4 + ty], stores[kind].at[own_part + i]
            if away:
                remote(src, dst, send_kv, got_direct.at[kind, i // 4], device(x, ty, tz, c)).start()
            else:
                pltpu.make_async_copy(src, dst, got_direct.at[kind, 0]).start()

        return step

    def send_far(kind, ref):
        def step(i, away):
            ty, tz = target(i)
            src, dst = ref.at[(1 - pair) * 16 + tz * 4 + ty], stores[kind].at[own_part + i]
            remote(src, dst, send_kv, got_direct.at[kind, i // 4], device(beside, ty, tz, c)).start()

        return step

    def send_own_queries(i, away):
        ty, tz = target(i)
        src = q_ref.at[pair * 16 + tz * 4 + ty]
        if away:
            remote(src, queries.at[16 + i], send_kv, got_queries.at[1 + i // 4], device(x, ty, tz, c)).start()
        else:
            pltpu.make_async_copy(src, queries.at[16], got_queries.at[1]).start()

    def send_far_queries(i, away):
        ty, tz = target(i)
        src = q_ref.at[(1 - pair) * 16 + tz * 4 + ty]
        remote(src, queries.at[i], send_kv, got_queries.at[0], device(beside, ty, tz, c)).start()

    def each_offset(*steps):
        for step in steps:
            step(0, False)

        def body(i, carry):
            for step in steps:
                step(i, True)
            return carry

        lax.fori_loop(1, 16, body, 0)

    stores = (own_k, own_v, far_k, far_v)
    arriving = (own_part, own_part, far_part, far_part)
    relaying = (far_part, far_part, own_part, own_part)
    pltpu.make_async_copy(lists_out.at[own_head], lists_in.at[16], got_lists).start()
    pl.semaphore_wait(barrier, 33)
    each_offset(send_own(OWN_K, k_ref))
    each_offset(send_lists_to)
    each_offset(send_far_queries, send_own(OWN_V, v_ref))

    def arrived(view, sem):
        pltpu.make_async_copy(view, view, sem).wait()

    def pass_on(kind, j):
        view = stores[kind].at[pl.ds(arriving[kind] + j * 4, 4)]
        arrived(view, got_direct.at[kind, j])
        remote(view, view, send_fwd, got_partner.at[kind, j], partner).start()
        remote(view, view, send_fwd, got_sibling.at[kind], sibling).start()

    def relay(kind, j):
        view = stores[kind].at[pl.ds(relaying[kind] + j * 4, 4)]
        arrived(view, got_partner.at[kind, j])
        remote(view, view, send_fwd, got_relayed.at[kind], sibling).start()

    def complete(kind):
        view = stores[kind].at[pl.ds(0, 16)]
        arrived(view, got_sibling.at[kind])
        arrived(view, got_relayed.at[kind])

    def attend(kind, shifts, events):
        def one(unit):
            query = queries[unit]
            running, found = None, []
            for cols in COLS:
                keys = jnp.concatenate([stores[kind][lists[unit, 0, bases[kind] + col]] for col in cols], 0)
                found.append(lax.dot_general(query, keys, NT, preferred_element_type=jnp.float32))
                for n in range(len(cols)):
                    piece = found[-1][:, n * BAND : (n + 1) * BAND]
                    running = piece if running is None else jnp.maximum(running, piece)
            shift = jnp.broadcast_to(jnp.max(running, -1, keepdims=True) * SCALE, (BAND, BAND))
            shifts[unit] = shift
            for cols, score in zip(COLS, found):
                weight = jnp.exp2(score * SCALE - jnp.concatenate([shift] * len(cols), 1))
                weights[unit, :, pl.ds(cols[0] * BAND, len(cols) * BAND)] = weight.astype(jnp.bfloat16)

        units(one, events)

    def mix(kind, finish, events, after=None):
        def one(unit):
            acc = None
            for cols in COLS:
                values = jnp.concatenate([stores[kind][lists[unit, 0, bases[kind] + col]] for col in cols], 0)
                values = jnp.concatenate([values, jnp.ones_like(values)], 1)
                weight = weights[unit, :, pl.ds(cols[0] * BAND, len(cols) * BAND)]
                product = jnp.dot(weight, values, preferred_element_type=jnp.float32)
                acc = product if acc is None else acc + product
            finish(unit, acc)

        units(one, events, after)

    def units(one, events, after=None):
        def body(i, carry):
            for at, event in events:
                pl.when(i == at)(event)
            for n in range(STEP):
                one(i * STEP + n)
            if after is not None:
                for n in range(STEP):
                    after(i * STEP + n)
            return carry

        lax.fori_loop(0, 32 // STEP, body, 0)

    def passing(at, kind, j):
        return at, functools.partial(pass_on, kind, j)

    def relaying_at(at, kind, j):
        return at, functools.partial(relay, kind, j)

    bases = (pair * PER, pair * PER, (1 - pair) * PER, (1 - pair) * PER)
    for j in range(4):
        pass_on(OWN_K, j)
    each_offset(send_far(FAR_K, k_ref), send_own_queries)
    each_offset(send_far(FAR_V, v_ref))
    for j in range(3):
        pass_on(OWN_V, j)
        relay(OWN_K, j)
    arrived(lists_in, got_lists)
    copy_lists = pltpu.make_async_copy(lists_in, lists, lists_sem)
    copy_lists.start()
    copy_lists.wait()
    pass_on(OWN_V, 3)
    relay(OWN_K, 3)
    arrived(queries.at[pl.ds(0, 16)], got_queries.at[0])
    complete(OWN_K)

    def more_queries(at, j):
        return at, lambda: arrived(queries.at[pl.ds(16 + j * 4, 4)], got_queries.at[1 + j])

    attend(
        OWN_K,
        max_own,
        [
            passing(1, FAR_K, 0), relaying_at(1, OWN_V, 0), more_queries(2, 0), passing(2, FAR_K, 1), more_queries(2, 1),
            relaying_at(2, OWN_V, 1), passing(3, FAR_K, 2), more_queries(3, 2), relaying_at(3, OWN_V, 2),
            more_queries(3, 3), relaying_at(3, OWN_V, 3),
        ],
    )
    complete(OWN_V)

    def keep(unit, acc):
        acc_own[unit] = acc

    mix(
        OWN_V,
        keep,
        [
            passing(0, FAR_K, 3), relaying_at(1, FAR_K, 0), passing(2, FAR_V, 0), relaying_at(2, FAR_K, 1),
            passing(3, FAR_V, 1), relaying_at(3, FAR_K, 2),
        ],
    )
    pass_on(FAR_V, 2)
    pass_on(FAR_V, 3)
    relay(FAR_K, 3)
    complete(FAR_K)
    attend(
        FAR_K,
        max_far,
        [relaying_at(1, FAR_V, 0), relaying_at(2, FAR_V, 1), relaying_at(3, FAR_V, 2)],
    )
    relay(FAR_V, 3)
    complete(FAR_V)

    def merge(unit, acc):
        first, shift, first_shift = acc_own[unit], max_far[unit], max_own[unit]
        joint = jnp.maximum(shift, first_shift)
        now, before = jnp.exp2(shift - joint), jnp.exp2(first_shift - joint)
        top = acc[:, :WIDTH] * now + first[:, :WIDTH] * before
        bottom = acc[:, WIDTH:] * now + first[:, WIDTH:] * before
        mixed[unit] = (top / bottom).astype(jnp.bfloat16)

    def give_back(unit):
        i = unit % 16
        dy = i % 4
        dz = (i // 4 + dy) % 4
        plane = jnp.where(unit < 16, beside, x)

        @pl.when(unit == 16)
        def _():
            pltpu.make_async_copy(mixed.at[16], o_ref.at[own_head], got_out).start()

        @pl.when(unit != 16)
        def _():
            remote(
                mixed.at[unit], o_ref.at[own_head], send_out, got_out,
                device(plane, (y - dy + 4) % 4, (z - dz + 4) % 4, c),
            ).start()

    mix(FAR_V, merge, [], give_back)

    def sent(view, sem):
        pltpu.make_async_copy(view, view, sem).wait()

    arrived(o_ref, got_out)
    sent(o_ref.at[pl.ds(0, 31)], send_out)
    sent(lists_out.at[pl.ds(0, 31)], send_lists)
    for store in stores[:2]:
        sent(store.at[pl.ds(0, 31)], send_kv)
    sent(queries.at[pl.ds(0, 31)], send_kv)
    for store in stores:
        sent(store.at[pl.ds(0, 48)], send_fwd)


def on_device(queries, keys, values, tiles):
    dma = pltpu.SemaphoreType.DMA
    any_space = pl.BlockSpec(memory_space=pl.ANY)
    bf16, f32 = jnp.bfloat16, jnp.float32
    return pl.pallas_call(
        kernel,
        out_shape=jax.ShapeDtypeStruct((HEADS, BAND, WIDTH), bf16),
        in_specs=[any_space, any_space, any_space, pl.BlockSpec(memory_space=pltpu.VMEM)],
        out_specs=any_space,
        scratch_shapes=[
            pltpu.VMEM((64, BAND, WIDTH), bf16),
            pltpu.VMEM((64, BAND, WIDTH), bf16),
            pltpu.VMEM((64, BAND, WIDTH), bf16),
            pltpu.VMEM((64, BAND, WIDTH), bf16),
            pltpu.VMEM((32, BAND, WIDTH), bf16),
            pltpu.VMEM((HEADS, 1, 128), jnp.int32),
            pltpu.VMEM((32, 1, 128), jnp.int32),
            pltpu.SMEM((32, 1, 128), jnp.int32),
            pltpu.VMEM((32, BAND, PER * BAND), bf16),
            pltpu.VMEM((32, BAND, 2 * WIDTH), f32),
            pltpu.VMEM((32, BAND, BAND), f32),
            pltpu.VMEM((32, BAND, BAND), f32),
            pltpu.VMEM((32, BAND, WIDTH), bf16),
            dma, dma, dma, dma,
            dma((4, 4)), dma((4, 4)), dma((4,)), dma((4,)), dma((5,)), dma, dma, dma,
        ],
        compiler_params=pltpu.CompilerParams(collective_id=0, has_side_effects=True, vmem_limit_bytes=52 * 2**20),
        cost_estimate=pl.CostEstimate(flops=10_200_000_000, bytes_accessed=4 * 2**20, transcendentals=20_000_000),
        name="attend_listed",
    )(queries, keys, values, tiles)


def solution(mesh):
    return jax.shard_map(
        on_device,
        mesh=mesh,
        in_specs=(
            P(None, ("grp", "seq"), None),
            P(None, ("grp", "seq"), None),
            P(None, ("grp", "seq"), None),
            P(("grp", "seq"), None, None),
        ),
        out_specs=P(None, ("grp", "seq"), None),
        check_vma=False,
    )
```

time: 106 us -> 90.8 us (0.86)
  Pallas kernels: 104 us -> 89 us
    pallas_call x1, Pallas kernels: 104 us -> 89 us  [on_device(): pl.pallas_call(kernel, out_shape=jax.ShapeDtypeStruct((HEADS, BAND, WIDTH...]
where the time goes in v2:
time: 90.8 us; the launch traced here: 90.7 us
  Pallas kernels  89 us (98%)
  local copies, waits for them, and re-layouts  1.69 us (2%)
    pallas_call x1, Pallas kernels, on_device(): pl.pallas_call(kernel, out_shape=jax.ShapeDtypeStruct((HEADS, BAND, WIDTH...  89 us

profile of v2, /device:TPU:1, one launch (start us, length us, event | category | flops | bytes accessed | tf_op | source)
XLA Modules:
  0.0 90.7 jit_solution(4946998293645643128)
XLA Ops:
  0.0 0.0 copy-start
  0.0 0.7 copy-done
  0.7 89.0 %attend_listed.1 = bf16[32,128,128]{2,1,0:T(8,128)(2,1)S(1)} custom-call(bf16[32,128,128]{2,1,0:T(8,128)(2,1)} %q_ref.1, bf16[32,128,128]{2,1,0:T(8,128)(2,1)} %k_ref.1, bf16[32,128,128]{2,1,0:T(8,128)(2,1)} %v_ref.1, s32[1,32,38]{2,1,0:T(8,128)S(1)} %copy-done), custom_call_target="tpu_custom_call" | custom-call | flops 10200000512 | bytes 4194304 | tf_op jit(solution)/shard_map/attend_listed/pallas_call | solution.py:311
  89.7 1.0 %copy.6 = bf16[32,128,128]{2,1,0:T(8,128)(2,1)} copy(bf16[32,128,128]{2,1,0:T(8,128)(2,1)S(1)} %attend_listed.1) | data formatting | bytes 2097152
Async XLA Ops:
  0.0 0.7 copy-start

commit v3 on v2

--- a/solution.py
+++ b/solution.py
@@ -25,7 +25,7 @@
 
 def kernel(
     q_ref, k_ref, v_ref, tiles_ref, o_ref,
-    own_k, own_v, far_k, far_v, queries, lists_out, lists_in, lists, weights, acc_own, max_own, max_far, mixed,
+    own_k, own_v, far_k, far_v, queries, lists_out, lists_in, lists, weights_own, weights_far, acc_own, max_own,
     send_kv, send_lists, send_fwd, send_out,
     got_direct, got_partner, got_sibling, got_relayed, got_queries, got_lists, got_out, lists_sem,
 ):
@@ -79,14 +79,14 @@
             src_ref=src, dst_ref=dst, send_sem=send_sem, recv_sem=recv_sem, device_id=device_id, device_id_type=MESH
         )
 
-    def send_lists_to(i, own):
+    def send_lists_to(i, away):
         ty, tz = target(i)
-        if own:
+        if away:
             remote(
-                lists_out.at[pair * 16 + tz * 4 + ty], lists_in.at[16 + i], send_lists, got_lists, device(x, ty, tz, c)
+                lists_out.at[pair * 16 + tz * 4 + ty], lists_in.at[i], send_lists, got_lists, device(x, ty, tz, c)
             ).start()
         remote(
-            lists_out.at[(1 - pair) * 16 + tz * 4 + ty], lists_in.at[i], send_lists, got_lists, device(beside, ty, tz, c)
+            lists_out.at[(1 - pair) * 16 + tz * 4 + ty], lists_in.at[16 + i], send_lists, got_lists, device(beside, ty, tz, c)
         ).start()
 
     def send_own(kind, ref):
@@ -112,34 +112,33 @@
         ty, tz = target(i)
         src = q_ref.at[pair * 16 + tz * 4 + ty]
         if away:
-            remote(src, queries.at[16 + i], send_kv, got_queries.at[1 + i // 4], device(x, ty, tz, c)).start()
+            remote(src, queries.at[i], send_kv, got_queries.at[i // 4], device(x, ty, tz, c)).start()
         else:
-            pltpu.make_async_copy(src, queries.at[16], got_queries.at[1]).start()
+            pltpu.make_async_copy(src, queries.at[0], got_queries.at[0]).start()
 
     def send_far_queries(i, away):
         ty, tz = target(i)
         src = q_ref.at[(1 - pair) * 16 + tz * 4 + ty]
-        remote(src, queries.at[i], send_kv, got_queries.at[0], device(beside, ty, tz, c)).start()
-
-    def each_offset(*steps):
-        for step in steps:
-            step(0, False)
+        remote(src, queries.at[16 + i], send_kv, got_queries.at[4 + i // 4], device(beside, ty, tz, c)).start()
+
+    def offsets(first, last, *steps):
+        if first == 0:
+            for step in steps:
+                step(0, False)
 
         def body(i, carry):
             for step in steps:
                 step(i, True)
             return carry
 
-        lax.fori_loop(1, 16, body, 0)
+        lax.fori_loop(max(first, 1), last, body, 0)
 
     stores = (own_k, own_v, far_k, far_v)
     arriving = (own_part, own_part, far_part, far_part)
     relaying = (far_part, far_part, own_part, own_part)
-    pltpu.make_async_copy(lists_out.at[own_head], lists_in.at[16], got_lists).start()
+    pltpu.make_async_copy(lists_out.at[own_head], lists_in.at[0], got_lists).start()
     pl.semaphore_wait(barrier, 33)
-    each_offset(send_own(OWN_K, k_ref))
-    each_offset(send_lists_to)
-    each_offset(send_far_queries, send_own(OWN_V, v_ref))
+    offsets(0, 16, send_own(OWN_K, k_ref))
 
     def arrived(view, sem):
         pltpu.make_async_copy(view, view, sem).wait()
@@ -147,20 +146,22 @@
     def pass_on(kind, j):
         view = stores[kind].at[pl.ds(arriving[kind] + j * 4, 4)]
         arrived(view, got_direct.at[kind, j])
-        remote(view, view, send_fwd, got_partner.at[kind, j], partner).start()
-        remote(view, view, send_fwd, got_sibling.at[kind], sibling).start()
-
-    def relay(kind, j):
-        view = stores[kind].at[pl.ds(relaying[kind] + j * 4, 4)]
-        arrived(view, got_partner.at[kind, j])
-        remote(view, view, send_fwd, got_relayed.at[kind], sibling).start()
+        remote(view, view, send_fwd, got_partner.at[kind], partner).start()
+        if j == 3:
+            part = stores[kind].at[pl.ds(arriving[kind], 16)]
+            remote(part, part, send_fwd, got_sibling.at[kind], sibling).start()
+
+    def relay(kind):
+        part = stores[kind].at[pl.ds(relaying[kind], 16)]
+        arrived(part, got_partner.at[kind])
+        remote(part, part, send_fwd, got_relayed.at[kind], sibling).start()
 
     def complete(kind):
         view = stores[kind].at[pl.ds(0, 16)]
         arrived(view, got_sibling.at[kind])
         arrived(view, got_relayed.at[kind])
 
-    def attend(kind, shifts, events):
+    def attend(kind, weights, settle, events):
         def one(unit):
             query = queries[unit]
             running, found = None, []
@@ -170,15 +171,14 @@
                 for n in range(len(cols)):
                     piece = found[-1][:, n * BAND : (n + 1) * BAND]
                     running = piece if running is None else jnp.maximum(running, piece)
-            shift = jnp.broadcast_to(jnp.max(running, -1, keepdims=True) * SCALE, (BAND, BAND))
-            shifts[unit] = shift
+            shift = settle(unit, jnp.broadcast_to(jnp.max(running, -1, keepdims=True) * SCALE, (BAND, BAND)))
             for cols, score in zip(COLS, found):
                 weight = jnp.exp2(score * SCALE - jnp.concatenate([shift] * len(cols), 1))
                 weights[unit, :, pl.ds(cols[0] * BAND, len(cols) * BAND)] = weight.astype(jnp.bfloat16)
 
         units(one, events)
 
-    def mix(kind, finish, events, after=None):
+    def mix(kind, weights, finish, events, after=None):
         def one(unit):
             acc = None
             for cols in COLS:
@@ -195,11 +195,15 @@
         def body(i, carry):
             for at, event in events:
                 pl.when(i == at)(event)
-            for n in range(STEP):
-                one(i * STEP + n)
+            if after is None:
+                mine = [i * STEP + n for n in range(STEP)]
+            else:
+                mine = [i * (STEP // 2) + n // 2 + 16 * (1 - n % 2) for n in range(STEP)]
+            for unit in mine:
+                one(unit)
             if after is not None:
-                for n in range(STEP):
-                    after(i * STEP + n)
+                for unit in mine:
+                    after(unit)
             return carry
 
         lax.fori_loop(0, 32 // STEP, body, 0)
@@ -207,89 +211,109 @@
     def passing(at, kind, j):
         return at, functools.partial(pass_on, kind, j)
 
-    def relaying_at(at, kind, j):
-        return at, functools.partial(relay, kind, j)
+    def relaying_at(at, kind):
+        return at, functools.partial(relay, kind)
 
     bases = (pair * PER, pair * PER, (1 - pair) * PER, (1 - pair) * PER)
-    for j in range(4):
-        pass_on(OWN_K, j)
-    each_offset(send_far(FAR_K, k_ref), send_own_queries)
-    each_offset(send_far(FAR_V, v_ref))
-    for j in range(3):
+
+    def after_chunks(kind, *steps):
+        for j in range(4):
+            pass_on(kind, j)
+            offsets(4 * j, 4 * j + 4, *steps)
+
+    after_chunks(OWN_K, send_far(FAR_K, k_ref), send_own_queries)
+    offsets(0, 16, send_lists_to)
+
+    def next_far_keys(j):
+        pass_on(FAR_K, j)
+        offsets(4 * j, 4 * j + 4, send_far_queries, send_own(OWN_V, v_ref))
+
+    def next_own_values(j):
         pass_on(OWN_V, j)
-        relay(OWN_K, j)
+        offsets(4 * j, 4 * j + 4, send_far(FAR_V, v_ref))
+
+    def query_chunk(j):
+        arrived(queries.at[pl.ds(j * 4, 4)], got_queries.at[j])
+
+    def querying(at, j):
+        return at, functools.partial(query_chunk, j)
+
+    next_far_keys(0)
+    next_far_keys(1)
     arrived(lists_in, got_lists)
     copy_lists = pltpu.make_async_copy(lists_in, lists, lists_sem)
     copy_lists.start()
+    relay(OWN_K)
+    next_far_keys(2)
     copy_lists.wait()
-    pass_on(OWN_V, 3)
-    relay(OWN_K, 3)
-    arrived(queries.at[pl.ds(0, 16)], got_queries.at[0])
+    query_chunk(0)
+    query_chunk(1)
     complete(OWN_K)
 
-    def more_queries(at, j):
-        return at, lambda: arrived(queries.at[pl.ds(16 + j * 4, 4)], got_queries.at[1 + j])
+    def settle_own(unit, shift):
+        max_own[unit] = shift
+        return shift
+
+    def settle_far(unit, shift):
+        joint = jnp.maximum(shift, max_own[unit])
+        max_own[unit] = jnp.exp2(max_own[unit] - joint)
+        return joint
 
     attend(
         OWN_K,
-        max_own,
+        weights_own,
+        settle_own,
         [
-            passing(1, FAR_K, 0), relaying_at(1, OWN_V, 0), more_queries(2, 0), passing(2, FAR_K, 1), more_queries(2, 1),
-            relaying_at(2, OWN_V, 1), passing(3, FAR_K, 2), more_queries(3, 2), relaying_at(3, OWN_V, 2),
-            more_queries(3, 3), relaying_at(3, OWN_V, 3),
+            (0, functools.partial(next_far_keys, 3)), querying(1, 2), querying(1, 3),
+            (1, functools.partial(next_own_values, 0)), (1, functools.partial(next_own_values, 1)),
+            (2, functools.partial(next_own_values, 2)), querying(2, 4), querying(2, 5),
+            (3, functools.partial(next_own_values, 3)), querying(3, 6), querying(3, 7),
+        ],
+    )
+    pass_on(FAR_V, 0)
+    relay(FAR_K)
+    complete(FAR_K)
+    attend(
+        FAR_K,
+        weights_far,
+        settle_far,
+        [
+            passing(1, FAR_V, 1), passing(1, FAR_V, 2), passing(2, FAR_V, 3), relaying_at(3, OWN_V),
         ],
     )
     complete(OWN_V)
 
     def keep(unit, acc):
-        acc_own[unit] = acc
-
-    mix(
-        OWN_V,
-        keep,
-        [
-            passing(0, FAR_K, 3), relaying_at(1, FAR_K, 0), passing(2, FAR_V, 0), relaying_at(2, FAR_K, 1),
-            passing(3, FAR_V, 1), relaying_at(3, FAR_K, 2),
-        ],
-    )
-    pass_on(FAR_V, 2)
-    pass_on(FAR_V, 3)
-    relay(FAR_K, 3)
-    complete(FAR_K)
-    attend(
-        FAR_K,
-        max_far,
-        [relaying_at(1, FAR_V, 0), relaying_at(2, FAR_V, 1), relaying_at(3, FAR_V, 2)],
-    )
-    relay(FAR_V, 3)
+        factor = max_own[unit]
+        acc_own[unit] = (acc[:, :WIDTH] * factor).astype(jnp.bfloat16)
+        max_own[unit] = acc[:, WIDTH:] * factor
+
+    mix(OWN_V, weights_own, keep, [])
+    relay(FAR_V)
     complete(FAR_V)
 
     def merge(unit, acc):
-        first, shift, first_shift = acc_own[unit], max_far[unit], max_own[unit]
-        joint = jnp.maximum(shift, first_shift)
-        now, before = jnp.exp2(shift - joint), jnp.exp2(first_shift - joint)
-        top = acc[:, :WIDTH] * now + first[:, :WIDTH] * before
-        bottom = acc[:, WIDTH:] * now + first[:, WIDTH:] * before
-        mixed[unit] = (top / bottom).astype(jnp.bfloat16)
+        top, bottom = acc[:, :WIDTH] + acc_own[unit].astype(jnp.float32), acc[:, WIDTH:] + max_own[unit]
+        queries[unit] = (top / bottom).astype(jnp.bfloat16)
 
     def give_back(unit):
         i = unit % 16
         dy = i % 4
         dz = (i // 4 + dy) % 4
-        plane = jnp.where(unit < 16, beside, x)
-
-        @pl.when(unit == 16)
+        plane = jnp.where(unit < 16, x, beside)
+
+        @pl.when(unit == 0)
         def _():
-            pltpu.make_async_copy(mixed.at[16], o_ref.at[own_head], got_out).start()
-
-        @pl.when(unit != 16)
+            pltpu.make_async_copy(queries.at[0], o_ref.at[own_head], got_out).start()
+
+        @pl.when(unit != 0)
         def _():
             remote(
-                mixed.at[unit], o_ref.at[own_head], send_out, got_out,
+                queries.at[unit], o_ref.at[own_head], send_out, got_out,
                 device(plane, (y - dy + 4) % 4, (z - dz + 4) % 4, c),
             ).start()
 
-    mix(FAR_V, merge, [], give_back)
+    mix(FAR_V, weights_far, merge, [], give_back)
 
     def sent(view, sem):
         pltpu.make_async_copy(view, view, sem).wait()
@@ -323,12 +347,11 @@
             pltpu.VMEM((32, 1, 128), jnp.int32),
             pltpu.SMEM((32, 1, 128), jnp.int32),
             pltpu.VMEM((32, BAND, PER * BAND), bf16),
-            pltpu.VMEM((32, BAND, 2 * WIDTH), f32),
+            pltpu.VMEM((32, BAND, PER * BAND), bf16),
+            pltpu.VMEM((32, BAND, WIDTH), bf16),
             pltpu.VMEM((32, BAND, BAND), f32),
-            pltpu.VMEM((32, BAND, BAND), f32),
-            pltpu.VMEM((32, BAND, WIDTH), bf16),
             dma, dma, dma, dma,
-            dma((4, 4)), dma((4, 4)), dma((4,)), dma((4,)), dma((5,)), dma, dma, dma,
+            dma((4, 4)), dma((4,)), dma((4,)), dma((4,)), dma((8,)), dma, dma, dma,
         ],
         compiler_params=pltpu.CompilerParams(collective_id=0, has_side_effects=True, vmem_limit_bytes=52 * 2**20),
         cost_estimate=pl.CostEstimate(flops=10_200_000_000, bytes_accessed=4 * 2**20, transcendentals=20_000_000),

time: 90.8 us -> 89.2 us (0.982)
  Pallas kernels: 89 us -> 87.3 us
    pallas_call x1, Pallas kernels: 89 us -> 87.3 us  [on_device(): pl.pallas_call(kernel, out_shape=jax.ShapeDtypeStruct((HEADS, BAND, WIDTH...]
where the time goes in v3:
time: 89.2 us; the launch traced here: 89 us
  Pallas kernels  87.3 us (98%)
  local copies, waits for them, and re-layouts  1.69 us (2%)
    pallas_call x1, Pallas kernels, on_device(): pl.pallas_call(kernel, out_shape=jax.ShapeDtypeStruct((HEADS, BAND, WIDTH...  87.3 us

profile of v3, /device:TPU:1, one launch (start us, length us, event | category | flops | bytes accessed | tf_op | source)
XLA Modules:
  0.0 89.0 jit_solution(3061473783148543698)
XLA Ops:
  0.0 0.0 copy-start
  0.0 0.7 copy-done
  0.7 87.3 %attend_listed.1 = bf16[32,128,128]{2,1,0:T(8,128)(2,1)S(1)} custom-call(bf16[32,128,128]{2,1,0:T(8,128)(2,1)} %q_ref.1, bf16[32,128,128]{2,1,0:T(8,128)(2,1)} %k_ref.1, bf16[32,128,128]{2,1,0:T(8,128)(2,1)} %v_ref.1, s32[1,32,38]{2,1,0:T(8,128)S(1)} %copy-done), custom_call_target="tpu_custom_call" | custom-call | flops 10200000512 | bytes 4194304 | tf_op jit(solution)/shard_map/attend_listed/pallas_call | solution.py:335
  88.1 1.0 %copy.6 = bf16[32,128,128]{2,1,0:T(8,128)(2,1)} copy(bf16[32,128,128]{2,1,0:T(8,128)(2,1)S(1)} %attend_listed.1) | data formatting | bytes 2097152
Async XLA Ops:
  0.0 0.7 copy-start

commit v4 on v3

--- a/solution.py
+++ b/solution.py
@@ -192,13 +192,15 @@
         units(one, events, after)
 
     def units(one, events, after=None):
+        step = STEP if after is None else STEP // 2
+
         def body(i, carry):
             for at, event in events:
                 pl.when(i == at)(event)
             if after is None:
                 mine = [i * STEP + n for n in range(STEP)]
             else:
-                mine = [i * (STEP // 2) + n // 2 + 16 * (1 - n % 2) for n in range(STEP)]
+                mine = [i * (step // 2) + n // 2 + 16 * (1 - n % 2) for n in range(step)]
             for unit in mine:
                 one(unit)
             if after is not None:
@@ -206,7 +208,7 @@
                     after(unit)
             return carry
 
-        lax.fori_loop(0, 32 // STEP, body, 0)
+        lax.fori_loop(0, 32 // step, body, 0)
 
     def passing(at, kind, j):
         return at, functools.partial(pass_on, kind, j)

time: 89.2 us -> 88.5 us (level)
  no operation moved by 1% of the time
where the time goes in v4:
time: 88.5 us; the launch traced here: 88.4 us
  Pallas kernels  86.7 us (98%)
  local copies, waits for them, and re-layouts  1.69 us (2%)
    pallas_call x1, Pallas kernels, on_device(): pl.pallas_call(kernel, out_shape=jax.ShapeDtypeStruct((HEADS, BAND, WIDTH...  86.7 us

profile of v4, /device:TPU:1, one launch (start us, length us, event | category | flops | bytes accessed | tf_op | source)
XLA Modules:
  0.0 88.4 jit_solution(17474107580474858258)
XLA Ops:
  0.0 0.0 copy-start
  0.0 0.7 copy-done
  0.7 86.7 %attend_listed.1 = bf16[32,128,128]{2,1,0:T(8,128)(2,1)S(1)} custom-call(bf16[32,128,128]{2,1,0:T(8,128)(2,1)} %q_ref.1, bf16[32,128,128]{2,1,0:T(8,128)(2,1)} %k_ref.1, bf16[32,128,128]{2,1,0:T(8,128)(2,1)} %v_ref.1, s32[1,32,38]{2,1,0:T(8,128)S(1)} %copy-done), custom_call_target="tpu_custom_call" | custom-call | flops 10200000512 | bytes 4194304 | tf_op jit(solution)/shard_map/attend_listed/pallas_call | solution.py:337
  87.4 1.0 %copy.6 = bf16[32,128,128]{2,1,0:T(8,128)(2,1)} copy(bf16[32,128,128]{2,1,0:T(8,128)(2,1)S(1)} %attend_listed.1) | data formatting | bytes 2097152
Async XLA Ops:
  0.0 0.7 copy-start
